TPU v7x, 128 devices: a whole 4x4x4 slice. The times are simulated.
128 devices in a mesh: stn: 16 (over x, z_hi, core), chan: 8 (over z_lo, y).
Axes of the slice: x: 4, y: 4, z: 4 (z_hi: 2, z_lo: 2; z = z_hi * 2 + z_lo), core: 2. Of those that a mesh axis runs over, the one named last changes fastest.
Arguments:
- voltages: bfloat16 [256, 2, 512, 1024], P('stn', None, 'chan'), may hold values from -6 to 6
- taps: float32 [4, 512], replicated, may hold values from 0.25 to 1
- flags: int32 [256], P('stn'), may hold values 0 or 1
Outputs:
- stokes: float32 [512, 8, 256, 256], P('chan', None, 'stn')
Inputs may be any that keep to these rules, and one draw needn't show every extreme that they name: 1 keeps a station, 0 flags it.
All inputs are finite; a program needn't handle non-finite values. No bound on the sum of `flags` on one device may be relied on, other than what follows from the above.
Results may differ from a plain program's by a relative error of at most 0.0048.
Values may be sent and summed in bfloat16 or wider, within the bound.
A program may use at most 128 MiB of HBM per device.

v0:
```python
import functools
import math

import jax
import jax.numpy as jnp
import numpy as np
from jax import lax
from jax.experimental import pallas as pl
from jax.experimental.pallas import tpu as pltpu
from jax.sharding import PartitionSpec as P

CHANNELS = 512
TAPS = 4
LANES = 128
MESH = pl.DeviceIdType.MESH


def half_table(stn_count, chan_count):
    per_device = CHANNELS // (stn_count * chan_count)
    stn, chan, own = np.meshgrid(
        np.arange(stn_count), np.arange(chan_count), np.arange(per_device), indexing="ij"
    )
    rows = jnp.asarray((chan * stn_count * per_device + stn * per_device + own).reshape(-1), jnp.int32)
    samples = jnp.arange(CHANNELS, dtype=jnp.int32)
    angles = 2.0 * math.pi / CHANNELS * (rows[:, None] * samples[None, :] % CHANNELS).astype(jnp.float32)
    factor = 1.0 / math.sqrt(CHANNELS)
    table = jnp.concatenate([jnp.cos(angles) * factor, jnp.sin(angles) * factor], axis=1)
    return table.astype(jnp.bfloat16)


def kernel(
    volt_hbm, taps_ref, flags_ref, table_hbm, out_ref,
    volt, table, raw, mixed, planes, a_src, a_dst, terms, b_src, halo_src, halo_dst,
    load_sem, halo_sem, a_send, a_recv, b_send, b_recv,
):
    stn_count, chan_count = lax.axis_size("stn"), lax.axis_size("chan")
    count = stn_count * chan_count
    stn, chan = lax.axis_index("stn"), lax.axis_index("chan")
    me = stn * chan_count + chan
    feeds, steps = volt.shape[0], volt.shape[1]
    stations = feeds // 2
    pitch = steps + 8
    per_device = CHANNELS // count
    parts = load_sem.shape[0] - 1
    share = feeds // parts

    def owner(index):
        return (index // chan_count, index % chan_count)

    def partner(step):
        return (me + step) % count

    table_copy = pltpu.make_async_copy(table_hbm, table, load_sem.at[parts])
    for part in range(parts):
        span = pl.ds(part * share, share)
        pltpu.make_async_copy(volt_hbm.at[span], volt.at[span], load_sem.at[part]).start()
    table_copy.start()

    barrier = pltpu.get_barrier_semaphore()

    @pl.loop(1, count)
    def _(step):
        pl.semaphore_signal(barrier, inc=1, device_id=owner(partner(step)), device_id_type=MESH)

    for part in range(parts):
        span = pl.ds(part * share, share)
        pltpu.make_async_copy(volt_hbm.at[span], volt.at[span], load_sem.at[part]).wait()

        @pl.loop(part * share, (part + 1) * share)
        def _(feed):
            flag = flags_ref[feed // 2].astype(jnp.float32)
            for tile in range(8):
                block = volt[feed, :, tile * LANES : (tile + 1) * LANES].astype(jnp.float32) * flag
                raw[tile, pl.ds(pl.multiple_of(feed * pitch + 8, 8), steps), :] = block

    for tile in range(8):
        for back in range(TAPS - 1):
            rows = raw[tile, pl.ds(8 + steps - (TAPS - 1) + back, feeds, stride=pitch), :]
            halo_src[pl.ds(back * feeds, feeds), pl.ds(tile * LANES, LANES)] = rows.astype(jnp.bfloat16)

    def filtered(first):
        @pl.loop(0, feeds)
        def _(feed):
            station, polar = feed // 2, feed % 2
            for tile in range(8):
                weights = [
                    taps_ref[pl.ds(tap, 1), pl.ds((tile % 4) * LANES, LANES)] for tap in range(TAPS)
                ]
                rows = [
                    raw[tile, pl.ds(feed * pitch + 8 + first - 3 + shift, 8, stride=8), :]
                    for shift in range(7)
                ]
                sums = []
                for index in range(4):
                    total = weights[0] * rows[index]
                    for tap in range(1, TAPS):
                        total = total + weights[tap] * rows[index + tap]
                    sums.append(total)
                block = jnp.concatenate(sums, axis=0).astype(jnp.bfloat16)
                base = station * LANES + polar * 32
                mixed[pl.ds(pl.multiple_of(base, 32), 32), tile * LANES : (tile + 1) * LANES] = block
                other = (tile + 4) % 8
                turned = block if tile >= 4 else -block
                mixed[
                    pl.ds(pl.multiple_of(base + 64, 32), 32), other * LANES : (other + 1) * LANES
                ] = turned

    def transformed(half):
        @pl.loop(0, stations // 2)
        def _(pair):
            rows = mixed[pl.ds(pl.multiple_of(pair * 256, 256), 256), :]
            out = lax.dot_general(
                table[...], rows, (((1,), (1,)), ((), ())), preferred_element_type=jnp.float32
            )
            planes[pl.ds(2 * pair, CHANNELS, stride=stations), :] = out[:, :LANES]
            planes[pl.ds(2 * pair + 1, CHANNELS, stride=stations), :] = out[:, LANES:]

        depth = per_device * stations
        group = 8

        @pl.loop(0, count // group)
        def _(block):
            rows = planes[pl.ds(pl.multiple_of(block * (group * depth), group * depth), group * depth), :]
            a_src[half, pl.ds(block * group, group)] = rows.astype(jnp.bfloat16).reshape(group, depth, LANES)

    filtered(4)
    table_copy.wait()
    transformed(0)
    pl.semaphore_wait(barrier, count - 1)

    after = (stn, (chan + 1) % chan_count)
    halo_copy = pltpu.make_async_remote_copy(
        src_ref=halo_src, dst_ref=halo_dst, send_sem=halo_sem.at[0], recv_sem=halo_sem.at[1],
        device_id=after, device_id_type=MESH,
    )
    halo_copy.start()

    def a_copy(half, span, slot, index):
        return pltpu.make_async_remote_copy(
            src_ref=a_src.at[half, index, span], dst_ref=a_dst.at[half, me, span],
            send_sem=a_send.at[slot], recv_sem=a_recv.at[slot],
            device_id=owner(index), device_id_type=MESH,
        )

    def a_all(half, span, slot):
        ref = a_dst.at[half, pl.ds(0, count - 1), span]
        return pltpu.make_async_remote_copy(
            src_ref=ref, dst_ref=ref, send_sem=a_send.at[slot], recv_sem=a_recv.at[slot],
            device_id=owner(me), device_id_type=MESH,
        )

    whole = pl.ds(0, per_device * stations)
    halves = [pl.ds(part * 2 * stations, 2 * stations) for part in range(per_device // 2)]

    @pl.loop(1, count)
    def _(step):
        a_copy(0, whole, 0, partner(step)).start()

    a_dst[0, me] = a_src[0, me]

    halo_copy.wait()
    for tile in range(8):
        for back in range(TAPS - 1):
            rows = halo_dst[pl.ds(back * feeds, feeds), pl.ds(tile * LANES, LANES)].astype(jnp.float32)
            rows = jnp.where(chan == 0, 0.0, rows)
            raw[tile, pl.ds(8 - (TAPS - 1) + back, feeds, stride=pitch), :] = rows

    filtered(0)
    transformed(1)
    a_dst[1, me] = a_src[1, me]

    for part, span in enumerate(halves):
        @pl.loop(1, count)
        def _(step):
            a_copy(1, span, 1 + part, partner(step)).start()

    lane = lax.broadcasted_iota(jnp.int32, (1, LANES), 1)
    first_polar = lane % 64 < 32
    polar_sign = jnp.where(first_polar, 1.0, -1.0)
    turn_sign = jnp.where(lane < 64, 1.0, -1.0)
    rows_total = stn_count * stations

    def correlated(own):
        for half in range(2):
            @pl.loop(0, chan_count)
            def _(source):
                x = jnp.concatenate(
                    [
                        a_dst[half, block * chan_count + source, own * stations : (own + 1) * stations, :]
                        for block in range(stn_count)
                    ],
                    axis=0,
                ).astype(jnp.float32)
                swapped = jnp.where(first_polar, pltpu.roll(x, 96, 1), pltpu.roll(x, 32, 1))
                turned = pltpu.roll(x, 64, 1) * turn_sign
                both = pltpu.roll(swapped, 64, 1) * turn_sign
                values = [
                    x, turned, x * polar_sign, turned * polar_sign,
                    swapped, both, both * -polar_sign, swapped * polar_sign,
                ]
                lanes = pl.ds(pl.multiple_of((half * chan_count + source) * LANES, LANES), LANES)
                for index, value in enumerate(values):
                    terms[index * rows_total : (index + 1) * rows_total, lanes] = value.astype(jnp.bfloat16)

        @pl.loop(0, 4)
        def _(quarter):
            left = terms[pl.ds(pl.multiple_of(quarter * 2 * rows_total, 2 * rows_total), 2 * rows_total), :]
            out = lax.dot_general(
                left, terms[:rows_total, :], (((1,), (1,)), ((), ())), preferred_element_type=jnp.float32
            ).astype(jnp.bfloat16)
            for which in range(2):
                rows = out[which * rows_total : (which + 1) * rows_total]
                b_src[own, :, 2 * quarter + which] = rows.reshape(stn_count, stations, rows_total)

    for own in range(per_device):
        if own == 0:
            a_all(0, whole, 0).wait()
        if own % 2 == 0:
            a_all(1, halves[own // 2], 1 + own // 2).wait()
        correlated(own)

        @pl.loop(1, stn_count)
        def _(step):
            target = (stn + step) % stn_count
            pltpu.make_async_remote_copy(
                src_ref=b_src.at[own, target], dst_ref=out_ref.at[stn * per_device + own],
                send_sem=b_send, recv_sem=b_recv, device_id=(target, chan), device_id_type=MESH,
            ).start()

        out_ref[stn * per_device + own] = b_src[own, stn]

    ref = out_ref.at[pl.ds(0, (stn_count - 1) * per_device)]
    pltpu.make_async_remote_copy(
        src_ref=ref, dst_ref=ref, send_sem=b_send, recv_sem=b_recv,
        device_id=owner(me), device_id_type=MESH,
    ).wait()


def on_device(voltages, taps, flags):
    stn_count, chan_count = lax.axis_size("stn"), lax.axis_size("chan")
    count = stn_count * chan_count
    stations, polars, steps, width = voltages.shape
    feeds = stations * polars
    per_device = CHANNELS // count
    total = stn_count * stations
    vmem = pltpu.VMEM
    narrow = pl.pallas_call(
        kernel,
        out_shape=jax.ShapeDtypeStruct((CHANNELS // chan_count, 8, stations, total), jnp.bfloat16),
        in_specs=[
            pl.BlockSpec(memory_space=pl.ANY),
            pl.BlockSpec(memory_space=vmem),
            pl.BlockSpec(memory_space=pltpu.SMEM),
            pl.BlockSpec(memory_space=pl.ANY),
        ],
        out_specs=pl.BlockSpec(memory_space=vmem),
        scratch_shapes=[
            vmem((feeds, steps, width), jnp.bfloat16),
            vmem((CHANNELS, width), jnp.bfloat16),
            vmem((8, feeds * (steps + 8), LANES), jnp.float32),
            vmem((stations * LANES, width), jnp.bfloat16),
            vmem((CHANNELS * stations, LANES), jnp.float32),
            vmem((2, count, per_device * stations, LANES), jnp.bfloat16),
            vmem((2, count, per_device * stations, LANES), jnp.bfloat16),
            vmem((8 * total, 2 * chan_count * LANES), jnp.bfloat16),
            vmem((per_device, stn_count, 8, stations, total), jnp.bfloat16),
            vmem(((TAPS - 1) * feeds, width), jnp.bfloat16),
            vmem(((TAPS - 1) * feeds, width), jnp.bfloat16),
            pltpu.SemaphoreType.DMA((5,)),
            pltpu.SemaphoreType.DMA((2,)),
            pltpu.SemaphoreType.DMA((3,)),
            pltpu.SemaphoreType.DMA((3,)),
            pltpu.SemaphoreType.DMA,
            pltpu.SemaphoreType.DMA,
        ],
        compiler_params=pltpu.CompilerParams(
            collective_id=0, has_side_effects=True, vmem_limit_bytes=60 * 1024 * 1024
        ),
        name="correlate",
    )(voltages.reshape(feeds, steps, width), taps, flags, half_table(stn_count, chan_count))
    return narrow.astype(jnp.float32) * (1.0 / (steps * chan_count))


def solution(mesh):
    return jax.shard_map(
        on_device,
        mesh=mesh,
        in_specs=(P("stn", None, "chan", None), P(), P("stn")),
        out_specs=P("chan", None, "stn", None),
        check_vma=False,
    )
```

profile of v0, /device:TPU:1, one launch (start us, length us, event | category | flops | bytes accessed | tf_op | source)
XLA Modules:
  0.0 149.6 jit_solution(6212152970487798534)
XLA Ops:
  0.0 5.7 %multiply_convert_fusion.1 = (bf16[512,512]{1,0:T(8,128)(2,1)S(1)}, bf16[512,512]{1,0:T(8,128)(2,1)S(1)}) fusion(s32[512]{0:T(512)} %constant.23.clone), kind=kLoop, calls=%fused_computation.9 | loop fusion | flops 4718592 | bytes 1050624 | tf_op jit(solution)/shard_map/convert
  5.7 1.1 pad_maximum_fusion.table_hbm
  6.8 136.0 %correlate.1 = bf16[64,8,16,256]{3,2,1,0:T(8,128)(2,1)} custom-call(bf16[32,64,1024]{2,1,0:T(8,128)(2,1)} %bitcast.1, f32[4,512]{1,0:T(4,128)} %taps_ref.1, s32[16]{0:T(128)} %flags_ref.1, bf16[512,1024]{1,0:T(8,128)(2,1)} %pad_maximum_fusion.table_hbm), custom_call_target="tpu_custom_call" | custom-call | tf_op jit(solution)/shard_map/correlate/pallas_call | solution.py:247
  142.8 6.8 %convert_multiply_fusion = f32[64,8,16,256]{3,2,1,0:T(8,128)} fusion(bf16[64,8,16,256]{3,2,1,0:T(8,128)(2,1)} %correlate.1), kind=kLoop, calls=%fused_computation | loop fusion | flops 4194304 | bytes 12582912 | tf_op jit(solution)/shard_map/mul | solution.py:281
where the time goes:
time: 150 us
  Pallas kernels  136 us (91%)
  other arithmetic  13.6 us (9%)
    pallas_call x1, Pallas kernels, on_device(): pl.pallas_call(kernel, out_shape=jax.ShapeDtypeStruct((CHANNELS // chan_c...  136 us
    mul x1, other arithmetic, on_device(): return narrow.astype(jnp.float32) * (1.0 / (steps * chan_count))  6.83 us
    another operation x1, other arithmetic  5.68 us

commit v1 on v0

v1 whole, which is shorter than its diff:
```python
import functools
import math

import jax
import jax.numpy as jnp
import numpy as np
from jax import lax
from jax.experimental import pallas as pl
from jax.experimental.pallas import tpu as pltpu
from jax.sharding import PartitionSpec as P

CHANNELS = 512
TAPS = 4
LANES = 128
MESH = pl.DeviceIdType.MESH


def half_table(stn_count, chan_count):
    per_device = CHANNELS // (stn_count * chan_count)
    pair, stn, chan, own = np.meshgrid(
        np.arange(per_device // 2), np.arange(stn_count), np.arange(chan_count), np.arange(2), indexing="ij"
    )
    rows = (chan * stn_count * per_device + stn * per_device + pair * 2 + own).reshape(-1)
    turns = (rows[:, None] * np.arange(CHANNELS)[None, :] % CHANNELS).astype(np.float32)
    angles = np.float32(2.0 * math.pi / CHANNELS) * turns
    factor = np.float32(1.0 / math.sqrt(CHANNELS))
    table = np.concatenate([np.cos(angles) * factor, np.sin(angles) * factor], axis=1)
    return jnp.asarray(table.astype(jnp.bfloat16))


def kernel(
    volt_hbm, taps_ref, flags_ref, table_hbm, out_ref,
    volt, table, raw, mixed, planes, a_src, a_dst, terms, b_src, halo_src, halo_dst,
    load_sem, halo_send, halo_recv, a_send, a_recv, b_send, b_recv, own_sem,
):
    stn_count, chan_count = lax.axis_size("stn"), lax.axis_size("chan")
    count = stn_count * chan_count
    stn, chan = lax.axis_index("stn"), lax.axis_index("chan")
    me = stn * chan_count + chan
    feeds, steps = volt.shape[0], volt.shape[1]
    stations = feeds // 2
    pitch = steps + 8
    per_device = CHANNELS // count
    parts = load_sem.shape[0] - 1
    share = feeds // parts

    def owner(index):
        return (index // chan_count, index % chan_count)

    x, z, core, y = stn // 4, (stn // 2 % 2) * 2 + chan // 4, stn % 2, chan % 4
    along_x = [(x + step) % 4 * 32 for step in range(4)]
    along_y = [(y + step) % 4 for step in range(4)]

    def plane_of(outer):
        other_z = (z + outer + 1) % 4
        return other_z // 2 * 16 + other_z % 2 * 4 + (core + outer // 4) % 2 * 8

    def each_partner(act):
        @pl.loop(0, 8)
        def _(outer):
            base = plane_of(outer)
            for step_y in range(4):
                for step_x in range(4):
                    index = base + along_x[step_x] + along_y[step_y]
                    if step_x == 0 and step_y == 0:
                        pl.when(outer != 3)(functools.partial(act, index))
                    else:
                        act(index)

    table_copy = pltpu.make_async_copy(table_hbm, table, load_sem.at[parts])
    loads = []
    for part in range(parts):
        span = pl.ds(part * share, share)
        loads.append(pltpu.make_async_copy(volt_hbm.at[span], volt.at[span], load_sem.at[part]))
        loads[-1].start()
    table_copy.start()

    barrier = pltpu.get_barrier_semaphore()

    def greet(index):
        pl.semaphore_signal(barrier, inc=1, device_id=owner(index), device_id_type=MESH)

    for part in range(parts):
        loads[part].wait()

        @pl.loop(part * share, (part + 1) * share)
        def _(feed):
            base = plane_of(feed // 4) + (y + feed % 4) % 4
            pl.when(feed != 12)(functools.partial(greet, base + along_x[0]))
            for step_x in range(1, 4):
                greet(base + along_x[step_x])
            flag = flags_ref[feed // 2].astype(jnp.float32)
            for tile in range(8):
                block = volt[feed, :, tile * LANES : (tile + 1) * LANES].astype(jnp.float32) * flag
                raw[tile, pl.ds(pl.multiple_of(feed * pitch + 8, 8), steps), :] = block

    for tile in range(8):
        for back in range(TAPS - 1):
            rows = raw[tile, pl.ds(8 + steps - (TAPS - 1) + back, feeds, stride=pitch), :]
            halo_src[pl.ds(back * feeds, feeds), pl.ds(tile * LANES, LANES)] = rows.astype(jnp.bfloat16)

    def filtered(half):
        first = 4 - 4 * half

        @pl.loop(0, feeds)
        def _(feed):
            station, polar = feed // 2, feed % 2
            for tile in range(8):
                weights = [
                    taps_ref[pl.ds(tap, 1), pl.ds((tile % 4) * LANES, LANES)] for tap in range(TAPS)
                ]
                rows = [
                    raw[tile, pl.ds(feed * pitch + 8 + first - 3 + shift, 8, stride=8), :]
                    for shift in range(7)
                ]
                sums = []
                for index in range(4):
                    total = weights[0] * rows[index]
                    for tap in range(1, TAPS):
                        total = total + weights[tap] * rows[index + tap]
                    sums.append(total)
                block = jnp.concatenate(sums, axis=0).astype(jnp.bfloat16)
                base = station * LANES + polar * 32
                mixed[
                    half, pl.ds(pl.multiple_of(base, 32), 32), tile * LANES : (tile + 1) * LANES
                ] = block
                other = (tile + 4) % 8
                turned = block if tile >= 4 else -block
                mixed[
                    half, pl.ds(pl.multiple_of(base + 64, 32), 32), other * LANES : (other + 1) * LANES
                ] = turned

    depth = 2 * stations

    def transformed(half, pair):
        @pl.loop(0, stations // 2)
        def _(both):
            rows = mixed[half, pl.ds(pl.multiple_of(both * 256, 256), 256), :]
            out = lax.dot_general(
                table[pair * 2 * count : (pair + 1) * 2 * count, :], rows,
                (((1,), (1,)), ((), ())), preferred_element_type=jnp.float32,
            )
            planes[pl.ds(2 * both, 2 * count, stride=stations), :] = out[:, :LANES]
            planes[pl.ds(2 * both + 1, 2 * count, stride=stations), :] = out[:, LANES:]

        group = 16
        slot = 2 * pair + half

        @pl.loop(0, count // group)
        def _(block):
            rows = planes[pl.ds(pl.multiple_of(block * (group * depth), group * depth), group * depth), :]
            a_src[slot, pl.ds(block * group, group)] = rows.astype(jnp.bfloat16).reshape(group, depth, LANES)

    def send_spectra(half, pair):
        slot = 2 * pair + half

        @each_partner
        def _(index):
            pltpu.make_async_remote_copy(
                src_ref=a_src.at[slot, index], dst_ref=a_dst.at[slot, me],
                send_sem=a_send.at[slot], recv_sem=a_recv.at[slot],
                device_id=owner(index), device_id_type=MESH,
            ).start()

        a_dst[slot, me] = a_src[slot, me]

    def await_spectra(half, pair):
        slot = 2 * pair + half
        ref = a_dst.at[slot, pl.ds(0, count - 1)]
        pltpu.make_async_remote_copy(
            src_ref=ref, dst_ref=ref, send_sem=a_send.at[slot], recv_sem=a_recv.at[slot],
            device_id=owner(me), device_id_type=MESH,
        ).wait()

    filtered(0)
    pl.semaphore_wait(barrier, count - 1)

    halo = []
    for back in range(TAPS - 1):
        span = pl.ds(back * feeds, feeds)
        halo.append(
            pltpu.make_async_remote_copy(
                src_ref=halo_src.at[span], dst_ref=halo_dst.at[span],
                send_sem=halo_send.at[back], recv_sem=halo_recv.at[back],
                device_id=(stn, (chan + 1) % chan_count), device_id_type=MESH,
            )
        )
        halo[-1].start()

    table_copy.wait()
    transformed(0, 0)
    send_spectra(0, 0)

    for copy in halo:
        copy.wait()
    for tile in range(8):
        for back in range(TAPS - 1):
            rows = halo_dst[pl.ds(back * feeds, feeds), pl.ds(tile * LANES, LANES)].astype(jnp.float32)
            rows = jnp.where(chan == 0, 0.0, rows)
            raw[tile, pl.ds(8 - (TAPS - 1) + back, feeds, stride=pitch), :] = rows

    filtered(1)
    transformed(1, 0)
    send_spectra(1, 0)
    transformed(0, 1)
    send_spectra(0, 1)
    transformed(1, 1)
    send_spectra(1, 1)

    lane = lax.broadcasted_iota(jnp.int32, (1, LANES), 1)
    first_polar = lane % 64 < 32
    polar_sign = jnp.where(first_polar, 1.0, -1.0)
    turn_sign = jnp.where(lane < 64, 1.0, -1.0)
    rows_total = stn_count * stations

    def correlated(own):
        for half in range(2):
            @pl.loop(0, chan_count)
            def _(source):
                x = jnp.concatenate(
                    [
                        a_dst[
                            2 * (own // 2) + half, block * chan_count + source,
                            own % 2 * stations : (own % 2 + 1) * stations, :,
                        ]
                        for block in range(stn_count)
                    ],
                    axis=0,
                ).astype(jnp.float32)
                swapped = jnp.where(first_polar, pltpu.roll(x, 96, 1), pltpu.roll(x, 32, 1))
                turned = pltpu.roll(x, 64, 1) * turn_sign
                both = pltpu.roll(swapped, 64, 1) * turn_sign
                values = [
                    x, turned, x * polar_sign, turned * polar_sign,
                    swapped, both, both * -polar_sign, swapped * polar_sign,
                ]
                lanes = pl.ds(pl.multiple_of((half * chan_count + source) * LANES, LANES), LANES)
                for index, value in enumerate(values):
                    terms[index * rows_total : (index + 1) * rows_total, lanes] = value.astype(jnp.bfloat16)

        @pl.loop(0, 4)
        def _(quarter):
            left = terms[pl.ds(pl.multiple_of(quarter * 2 * rows_total, 2 * rows_total), 2 * rows_total), :]
            out = lax.dot_general(
                left, terms[:rows_total, :], (((1,), (1,)), ((), ())), preferred_element_type=jnp.float32
            ).astype(jnp.bfloat16)
            for which in range(2):
                rows = out[which * rows_total : (which + 1) * rows_total]
                b_src[own, :, 2 * quarter + which] = rows.reshape(stn_count, stations, rows_total)

    own_copies = []
    for own in range(per_device):
        if own % 2 == 0:
            await_spectra(0, own // 2)
            await_spectra(1, own // 2)
        correlated(own)

        @pl.loop(1, stn_count)
        def _(step):
            target = (stn + step) % stn_count
            pltpu.make_async_remote_copy(
                src_ref=b_src.at[own, target], dst_ref=out_ref.at[stn * per_device + own],
                send_sem=b_send, recv_sem=b_recv, device_id=(target, chan), device_id_type=MESH,
            ).start()

        own_copies.append(
            pltpu.make_async_copy(b_src.at[own, stn], out_ref.at[stn * per_device + own], own_sem.at[own])
        )
        own_copies[-1].start()

    for copy in own_copies:
        copy.wait()
    ref = out_ref.at[pl.ds(0, (stn_count - 1) * per_device)]
    pltpu.make_async_remote_copy(
        src_ref=ref, dst_ref=ref, send_sem=b_send, recv_sem=b_recv,
        device_id=owner(me), device_id_type=MESH,
    ).wait()


def widen(scale, narrow_hbm, wide_hbm, narrow, wide, in_sem, out_sem):
    parts = in_sem.shape[0]
    share = narrow.shape[0] // parts
    spans = [pl.ds(part * share, share) for part in range(parts)]
    loads = [
        pltpu.make_async_copy(narrow_hbm.at[span], narrow.at[span], in_sem.at[part])
        for part, span in enumerate(spans)
    ]
    stores = [
        pltpu.make_async_copy(wide.at[span], wide_hbm.at[span], out_sem.at[part])
        for part, span in enumerate(spans)
    ]
    for load in loads:
        load.start()
    for part in range(parts):
        loads[part].wait()

        @pl.loop(part * share, (part + 1) * share)
        def _(row):
            wide[row] = narrow[row].astype(jnp.float32) * scale

        stores[part].start()
    for store in stores:
        store.wait()


def on_device(voltages, taps, flags):
    stn_count, chan_count = lax.axis_size("stn"), lax.axis_size("chan")
    count = stn_count * chan_count
    stations, polars, steps, width = voltages.shape
    feeds = stations * polars
    per_device = CHANNELS // count
    total = stn_count * stations
    vmem = pltpu.VMEM
    out_dims = (CHANNELS // chan_count, 8, stations, total)
    narrow = pl.pallas_call(
        kernel,
        out_shape=jax.ShapeDtypeStruct(out_dims, jnp.bfloat16),
        in_specs=[
            pl.BlockSpec(memory_space=pl.ANY),
            pl.BlockSpec(memory_space=vmem),
            pl.BlockSpec(memory_space=pltpu.SMEM),
            pl.BlockSpec(memory_space=pl.ANY),
        ],
        out_specs=pl.BlockSpec(memory_space=pl.ANY),
        scratch_shapes=[
            vmem((feeds, steps, width), jnp.bfloat16),
            vmem((CHANNELS, width), jnp.bfloat16),
            vmem((8, feeds * (steps + 8), LANES), jnp.float32),
            vmem((2, stations * LANES, width), jnp.bfloat16),
            vmem((2 * count * stations, LANES), jnp.float32),
            vmem((per_device, count, 2 * stations, LANES), jnp.bfloat16),
            vmem((per_device, count, 2 * stations, LANES), jnp.bfloat16),
            vmem((8 * total, 2 * chan_count * LANES), jnp.bfloat16),
            vmem((per_device, stn_count, 8, stations, total), jnp.bfloat16),
            vmem(((TAPS - 1) * feeds, width), jnp.bfloat16),
            vmem(((TAPS - 1) * feeds, width), jnp.bfloat16),
            pltpu.SemaphoreType.DMA((5,)),
            pltpu.SemaphoreType.DMA((TAPS - 1,)),
            pltpu.SemaphoreType.DMA((TAPS - 1,)),
            pltpu.SemaphoreType.DMA((per_device,)),
            pltpu.SemaphoreType.DMA((per_device,)),
            pltpu.SemaphoreType.DMA,
            pltpu.SemaphoreType.DMA,
            pltpu.SemaphoreType.DMA((per_device,)),
        ],
        compiler_params=pltpu.CompilerParams(
            collective_id=0, has_side_effects=True, vmem_limit_bytes=60 * 1024 * 1024
        ),
        name="correlate",
    )(voltages.reshape(feeds, steps, width), taps, flags, half_table(stn_count, chan_count))
    return pl.pallas_call(
        functools.partial(widen, 1.0 / (steps * chan_count)),
        out_shape=jax.ShapeDtypeStruct(out_dims, jnp.float32),
        in_specs=[pl.BlockSpec(memory_space=pl.ANY)],
        out_specs=pl.BlockSpec(memory_space=pl.ANY),
        scratch_shapes=[
            vmem(out_dims, jnp.bfloat16),
            vmem(out_dims, jnp.float32),
            pltpu.SemaphoreType.DMA((16,)),
            pltpu.SemaphoreType.DMA((16,)),
        ],
        compiler_params=pltpu.CompilerParams(vmem_limit_bytes=60 * 1024 * 1024),
        name="widen",
    )(narrow)


def solution(mesh):
    return jax.shard_map(
        on_device,
        mesh=mesh,
        in_specs=(P("stn", None, "chan", None), P(), P("stn")),
        out_specs=P("chan", None, "stn", None),
        check_vma=False,
    )
```

time: 150 us -> 124 us (0.83)
  the two profiles are of different devices: /device:TPU:1 before, /device:TPU:5 now
where the time goes in v1:
time: 124 us
  Pallas kernels  124 us (100%)
    pallas_call x1, Pallas kernels, on_device(): pl.pallas_call(kernel, out_shape=jax.ShapeDtypeStruct(out_dims, jnp.bfloa...  119 us
    pallas_call x1, Pallas kernels, on_device(): pl.pallas_call(functools.partial(widen, 1.0 / (steps * chan_count)), out_...  4.55 us

profile of v1, /device:TPU:5, one launch (start us, length us, event | category | flops | bytes accessed | tf_op | source)
XLA Modules:
  0.0 123.7 jit_solution(15796179917734256817)
XLA Ops:
  0.0 119.1 %correlate.1.narrow_hbm = bf16[64,8,16,256]{3,2,1,0:T(8,128)(2,1)} custom-call(bf16[32,64,1024]{2,1,0:T(8,128)(2,1)} %bitcast.1, f32[4,512]{1,0:T(4,128)} %taps_ref.1, s32[16]{0:T(128)} %flags_ref.1, bf16[512,1024]{1,0:T(8,128)(2,1)} %constant.2.clone.table_hbm), custom_call_target="tpu_custom_call" | custom-call | tf_op jit(solution)/shard_map/correlate/pallas_call | solution.py:315
  119.1 4.6 %widen.1 = f32[64,8,16,256]{3,2,1,0:T(8,128)} custom-call(bf16[64,8,16,256]{3,2,1,0:T(8,128)(2,1)} %correlate.1.narrow_hbm), custom_call_target="tpu_custom_call" | custom-call | tf_op jit(solution)/shard_map/widen/pallas_call | solution.py:351

commit v2 on v1

--- a/solution.py
+++ b/solution.py
@@ -80,15 +80,13 @@
     def greet(index):
         pl.semaphore_signal(barrier, inc=1, device_id=owner(index), device_id_type=MESH)
 
+    each_partner(greet)
+
     for part in range(parts):
         loads[part].wait()
 
         @pl.loop(part * share, (part + 1) * share)
         def _(feed):
-            base = plane_of(feed // 4) + (y + feed % 4) % 4
-            pl.when(feed != 12)(functools.partial(greet, base + along_x[0]))
-            for step_x in range(1, 4):
-                greet(base + along_x[step_x])
             flag = flags_ref[feed // 2].astype(jnp.float32)
             for tile in range(8):
                 block = volt[feed, :, tile * LANES : (tile + 1) * LANES].astype(jnp.float32) * flag
@@ -212,6 +210,7 @@
     polar_sign = jnp.where(first_polar, 1.0, -1.0)
     turn_sign = jnp.where(lane < 64, 1.0, -1.0)
     rows_total = stn_count * stations
+    targets = [(stn + step) % stn_count for step in range(1, stn_count)]
 
     def correlated(own):
         for half in range(2):
@@ -247,6 +246,13 @@
             for which in range(2):
                 rows = out[which * rows_total : (which + 1) * rows_total]
                 b_src[own, :, 2 * quarter + which] = rows.reshape(stn_count, stations, rows_total)
+            for which in range(2):
+                for target in targets:
+                    pltpu.make_async_remote_copy(
+                        src_ref=b_src.at[own, target, 2 * quarter + which],
+                        dst_ref=out_ref.at[stn * per_device + own, 2 * quarter + which],
+                        send_sem=b_send, recv_sem=b_recv, device_id=(target, chan), device_id_type=MESH,
+                    ).start()
 
     own_copies = []
     for own in range(per_device):
@@ -254,14 +260,6 @@
             await_spectra(0, own // 2)
             await_spectra(1, own // 2)
         correlated(own)
-
-        @pl.loop(1, stn_count)
-        def _(step):
-            target = (stn + step) % stn_count
-            pltpu.make_async_remote_copy(
-                src_ref=b_src.at[own, target], dst_ref=out_ref.at[stn * per_device + own],
-                send_sem=b_send, recv_sem=b_recv, device_id=(target, chan), device_id_type=MESH,
-            ).start()
 
         own_copies.append(
             pltpu.make_async_copy(b_src.at[own, stn], out_ref.at[stn * per_device + own], own_sem.at[own])

time: 124 us -> 120 us (0.968)
  the two profiles are of different devices: /device:TPU:5 before, /device:TPU:1 now
where the time goes in v2:
time: 120 us; the launch traced here: 119 us
  Pallas kernels  119 us (99%)
    pallas_call x1, Pallas kernels, on_device(): pl.pallas_call(kernel, out_shape=jax.ShapeDtypeStruct(out_dims, jnp.bfloa...  115 us
    pallas_call x1, Pallas kernels, on_device(): pl.pallas_call(functools.partial(widen, 1.0 / (steps * chan_count)), out_...  4.55 us

profile of v2, /device:TPU:1, one launch (start us, length us, event | category | flops | bytes accessed | tf_op | source)
XLA Modules:
  0.0 119.4 jit_solution(3403368151074137472)
XLA Ops:
  0.0 114.8 %correlate.1.narrow_hbm = bf16[64,8,16,256]{3,2,1,0:T(8,128)(2,1)} custom-call(bf16[32,64,1024]{2,1,0:T(8,128)(2,1)} %bitcast.1, f32[4,512]{1,0:T(4,128)} %taps_ref.1, s32[16]{0:T(128)} %flags_ref.1, bf16[512,1024]{1,0:T(8,128)(2,1)} %constant.2.clone.table_hbm), custom_call_target="tpu_custom_call" | custom-call | tf_op jit(solution)/shard_map/correlate/pallas_call | solution.py:313
  114.8 4.6 %widen.1 = f32[64,8,16,256]{3,2,1,0:T(8,128)} custom-call(bf16[64,8,16,256]{3,2,1,0:T(8,128)(2,1)} %correlate.1.narrow_hbm), custom_call_target="tpu_custom_call" | custom-call | tf_op jit(solution)/shard_map/widen/pallas_call | solution.py:349

commit v3 on v2

--- a/solution.py
+++ b/solution.py
@@ -170,9 +170,9 @@
             device_id=owner(me), device_id_type=MESH,
         ).wait()
 
-    filtered(0)
     pl.semaphore_wait(barrier, count - 1)
 
+    has_next, has_last = chan < chan_count - 1, chan > 0
     halo = []
     for back in range(TAPS - 1):
         span = pl.ds(back * feeds, feeds)
@@ -183,19 +183,32 @@
                 device_id=(stn, (chan + 1) % chan_count), device_id_type=MESH,
             )
         )
-        halo[-1].start()
-
+        pl.when(has_next)(halo[-1].start)
+
+    filtered(0)
     table_copy.wait()
     transformed(0, 0)
     send_spectra(0, 0)
 
     for copy in halo:
-        copy.wait()
-    for tile in range(8):
-        for back in range(TAPS - 1):
-            rows = halo_dst[pl.ds(back * feeds, feeds), pl.ds(tile * LANES, LANES)].astype(jnp.float32)
-            rows = jnp.where(chan == 0, 0.0, rows)
-            raw[tile, pl.ds(8 - (TAPS - 1) + back, feeds, stride=pitch), :] = rows
+        pl.when(has_next)(copy.wait_send)
+
+    @pl.when(has_last)
+    def _():
+        for copy in halo:
+            copy.wait_recv()
+        for tile in range(8):
+            for back in range(TAPS - 1):
+                rows = halo_dst[pl.ds(back * feeds, feeds), pl.ds(tile * LANES, LANES)]
+                raw[tile, pl.ds(8 - (TAPS - 1) + back, feeds, stride=pitch), :] = rows.astype(jnp.float32)
+
+    @pl.when(jnp.logical_not(has_last))
+    def _():
+        for tile in range(8):
+            for back in range(TAPS - 1):
+                raw[tile, pl.ds(8 - (TAPS - 1) + back, feeds, stride=pitch), :] = jnp.zeros(
+                    (feeds, LANES), jnp.float32
+                )
 
     filtered(1)
     transformed(1, 0)
@@ -275,28 +288,18 @@
     ).wait()
 
 
-def widen(scale, narrow_hbm, wide_hbm, narrow, wide, in_sem, out_sem):
-    parts = in_sem.shape[0]
+def widen(scale, narrow, wide_hbm, wide, out_sem):
+    parts = out_sem.shape[0]
     share = narrow.shape[0] // parts
-    spans = [pl.ds(part * share, share) for part in range(parts)]
-    loads = [
-        pltpu.make_async_copy(narrow_hbm.at[span], narrow.at[span], in_sem.at[part])
-        for part, span in enumerate(spans)
-    ]
-    stores = [
-        pltpu.make_async_copy(wide.at[span], wide_hbm.at[span], out_sem.at[part])
-        for part, span in enumerate(spans)
-    ]
-    for load in loads:
-        load.start()
+    stores = []
     for part in range(parts):
-        loads[part].wait()
-
         @pl.loop(part * share, (part + 1) * share)
         def _(row):
             wide[row] = narrow[row].astype(jnp.float32) * scale
 
-        stores[part].start()
+        span = pl.ds(part * share, share)
+        stores.append(pltpu.make_async_copy(wide.at[span], wide_hbm.at[span], out_sem.at[part]))
+        stores[-1].start()
     for store in stores:
         store.wait()
 
@@ -312,14 +315,14 @@
     out_dims = (CHANNELS // chan_count, 8, stations, total)
     narrow = pl.pallas_call(
         kernel,
-        out_shape=jax.ShapeDtypeStruct(out_dims, jnp.bfloat16),
+        out_shape=vmem(out_dims, jnp.bfloat16),
         in_specs=[
-            pl.BlockSpec(memory_space=pl.ANY),
+            pl.BlockSpec(memory_space=pltpu.HBM),
             pl.BlockSpec(memory_space=vmem),
             pl.BlockSpec(memory_space=pltpu.SMEM),
-            pl.BlockSpec(memory_space=pl.ANY),
+            pl.BlockSpec(memory_space=pltpu.HBM),
         ],
-        out_specs=pl.BlockSpec(memory_space=pl.ANY),
+        out_specs=pl.BlockSpec(memory_space=vmem),
         scratch_shapes=[
             vmem((feeds, steps, width), jnp.bfloat16),
             vmem((CHANNELS, width), jnp.bfloat16),
@@ -342,22 +345,20 @@
             pltpu.SemaphoreType.DMA((per_device,)),
         ],
         compiler_params=pltpu.CompilerParams(
-            collective_id=0, has_side_effects=True, vmem_limit_bytes=60 * 1024 * 1024
+            collective_id=0, has_side_effects=True, vmem_limit_bytes=50 * 1024 * 1024
         ),
         name="correlate",
     )(voltages.reshape(feeds, steps, width), taps, flags, half_table(stn_count, chan_count))
     return pl.pallas_call(
         functools.partial(widen, 1.0 / (steps * chan_count)),
         out_shape=jax.ShapeDtypeStruct(out_dims, jnp.float32),
-        in_specs=[pl.BlockSpec(memory_space=pl.ANY)],
+        in_specs=[pl.BlockSpec(memory_space=vmem)],
         out_specs=pl.BlockSpec(memory_space=pl.ANY),
         scratch_shapes=[
-            vmem(out_dims, jnp.bfloat16),
             vmem(out_dims, jnp.float32),
             pltpu.SemaphoreType.DMA((16,)),
-            pltpu.SemaphoreType.DMA((16,)),
         ],
-        compiler_params=pltpu.CompilerParams(vmem_limit_bytes=60 * 1024 * 1024),
+        compiler_params=pltpu.CompilerParams(vmem_limit_bytes=16 * 1024 * 1024),
         name="widen",
     )(narrow)
 

time: 120 us -> 114 us (0.950)
  Pallas kernels: 119 us -> 114 us
    pallas_call x1, Pallas kernels: 115 us -> 111 us  [on_device(): pl.pallas_call(kernel, out_shape=vmem(out_dims, jnp.bfloat16), in_specs=[...]
where the time goes in v3:
time: 114 us
  Pallas kernels  114 us (100%)
    pallas_call x1, Pallas kernels, on_device(): pl.pallas_call(kernel, out_shape=vmem(out_dims, jnp.bfloat16), in_specs=[...  111 us
    pallas_call x1, Pallas kernels, on_device(): pl.pallas_call(functools.partial(widen, 1.0 / (steps * chan_count)), out_...  3.46 us

profile of v3, /device:TPU:1, one launch (start us, length us, event | category | flops | bytes accessed | tf_op | source)
XLA Modules:
  0.0 114.1 jit_solution(12764714367973557504)
XLA Ops:
  0.0 110.6 %correlate.1.narrow = bf16[64,8,16,256]{3,2,1,0:T(8,128)(2,1)S(1)} custom-call(bf16[32,64,1024]{2,1,0:T(8,128)(2,1)} %bitcast.1, f32[4,512]{1,0:T(4,128)} %taps_ref.1, s32[16]{0:T(128)} %flags_ref.1, bf16[512,1024]{1,0:T(8,128)(2,1)} %constant.2.clone.table_hbm), custom_call_target="tpu_custom_call" | custom-call | tf_op jit(solution)/shard_map/correlate/pallas_call | solution.py:316
  110.6 3.5 %widen.1 = f32[64,8,16,256]{3,2,1,0:T(8,128)} custom-call(bf16[64,8,16,256]{3,2,1,0:T(8,128)(2,1)S(1)} %correlate.1.narrow), custom_call_target="tpu_custom_call" | custom-call | tf_op jit(solution)/shard_map/widen/pallas_call | solution.py:352

commit v4 on v3

--- a/solution.py
+++ b/solution.py
@@ -97,12 +97,10 @@
             rows = raw[tile, pl.ds(8 + steps - (TAPS - 1) + back, feeds, stride=pitch), :]
             halo_src[pl.ds(back * feeds, feeds), pl.ds(tile * LANES, LANES)] = rows.astype(jnp.bfloat16)
 
-    def filtered(half):
+    def filtered(half, both):
         first = 4 - 4 * half
-
-        @pl.loop(0, feeds)
-        def _(feed):
-            station, polar = feed // 2, feed % 2
+        for feed_of in range(4):
+            feed = 4 * both + feed_of
             for tile in range(8):
                 weights = [
                     taps_ref[pl.ds(tap, 1), pl.ds((tile % 4) * LANES, LANES)] for tap in range(TAPS)
@@ -118,7 +116,7 @@
                         total = total + weights[tap] * rows[index + tap]
                     sums.append(total)
                 block = jnp.concatenate(sums, axis=0).astype(jnp.bfloat16)
-                base = station * LANES + polar * 32
+                base = both * 2 * LANES + feed_of // 2 * LANES + feed_of % 2 * 32
                 mixed[
                     half, pl.ds(pl.multiple_of(base, 32), 32), tile * LANES : (tile + 1) * LANES
                 ] = block
@@ -130,17 +128,16 @@
 
     depth = 2 * stations
 
-    def transformed(half, pair):
-        @pl.loop(0, stations // 2)
-        def _(both):
-            rows = mixed[half, pl.ds(pl.multiple_of(both * 256, 256), 256), :]
-            out = lax.dot_general(
-                table[pair * 2 * count : (pair + 1) * 2 * count, :], rows,
-                (((1,), (1,)), ((), ())), preferred_element_type=jnp.float32,
-            )
-            planes[pl.ds(2 * both, 2 * count, stride=stations), :] = out[:, :LANES]
-            planes[pl.ds(2 * both + 1, 2 * count, stride=stations), :] = out[:, LANES:]
-
+    def transformed(half, pair, both):
+        rows = mixed[half, pl.ds(pl.multiple_of(both * 256, 256), 256), :]
+        out = lax.dot_general(
+            table[pair * 2 * count : (pair + 1) * 2 * count, :], rows,
+            (((1,), (1,)), ((), ())), preferred_element_type=jnp.float32,
+        )
+        planes[pl.ds(2 * both, 2 * count, stride=stations), :] = out[:, :LANES]
+        planes[pl.ds(2 * both + 1, 2 * count, stride=stations), :] = out[:, LANES:]
+
+    def packed(half, pair):
         group = 16
         slot = 2 * pair + half
 
@@ -148,6 +145,25 @@
         def _(block):
             rows = planes[pl.ds(pl.multiple_of(block * (group * depth), group * depth), group * depth), :]
             a_src[slot, pl.ds(block * group, group)] = rows.astype(jnp.bfloat16).reshape(group, depth, LANES)
+
+    def first_spectra(half):
+        last = stations // 2 - 1
+        filtered(half, 0)
+
+        @pl.loop(0, last)
+        def _(both):
+            transformed(half, 0, both)
+            filtered(half, both + 1)
+
+        transformed(half, 0, last)
+        packed(half, 0)
+
+    def second_spectra(half):
+        @pl.loop(0, stations // 2)
+        def _(both):
+            transformed(half, 1, both)
+
+        packed(half, 1)
 
     def send_spectra(half, pair):
         slot = 2 * pair + half
@@ -185,9 +201,8 @@
         )
         pl.when(has_next)(halo[-1].start)
 
-    filtered(0)
     table_copy.wait()
-    transformed(0, 0)
+    first_spectra(0)
     send_spectra(0, 0)
 
     for copy in halo:
@@ -210,60 +225,64 @@
                     (feeds, LANES), jnp.float32
                 )
 
-    filtered(1)
-    transformed(1, 0)
+    first_spectra(1)
     send_spectra(1, 0)
-    transformed(0, 1)
+    second_spectra(0)
     send_spectra(0, 1)
-    transformed(1, 1)
+    second_spectra(1)
     send_spectra(1, 1)
 
     lane = lax.broadcasted_iota(jnp.int32, (1, LANES), 1)
-    first_polar = lane % 64 < 32
-    polar_sign = jnp.where(first_polar, 1.0, -1.0)
+    first_part = lane % 64 < 32
     turn_sign = jnp.where(lane < 64, 1.0, -1.0)
     rows_total = stn_count * stations
     targets = [(stn + step) % stn_count for step in range(1, stn_count)]
 
     def correlated(own):
         for half in range(2):
-            @pl.loop(0, chan_count)
-            def _(source):
-                x = jnp.concatenate(
-                    [
-                        a_dst[
-                            2 * (own // 2) + half, block * chan_count + source,
-                            own % 2 * stations : (own % 2 + 1) * stations, :,
-                        ]
-                        for block in range(stn_count)
-                    ],
-                    axis=0,
-                ).astype(jnp.float32)
-                swapped = jnp.where(first_polar, pltpu.roll(x, 96, 1), pltpu.roll(x, 32, 1))
-                turned = pltpu.roll(x, 64, 1) * turn_sign
-                both = pltpu.roll(swapped, 64, 1) * turn_sign
-                values = [
-                    x, turned, x * polar_sign, turned * polar_sign,
-                    swapped, both, both * -polar_sign, swapped * polar_sign,
+            @pl.loop(0, chan_count // 2)
+            def _(couple):
+                first, second = (
+                    jnp.concatenate(
+                        [
+                            a_dst[
+                                2 * (own // 2) + half, block * chan_count + 2 * couple + source,
+                                own % 2 * stations : (own % 2 + 1) * stations, :,
+                            ]
+                            for block in range(stn_count)
+                        ],
+                        axis=0,
+                    ).astype(jnp.float32)
+                    for source in range(2)
+                )
+                polars = [
+                    jnp.where(first_part, first, pltpu.roll(second, 32, 1)),
+                    jnp.where(first_part, pltpu.roll(first, 96, 1), second),
                 ]
-                lanes = pl.ds(pl.multiple_of((half * chan_count + source) * LANES, LANES), LANES)
-                for index, value in enumerate(values):
-                    terms[index * rows_total : (index + 1) * rows_total, lanes] = value.astype(jnp.bfloat16)
-
-        @pl.loop(0, 4)
-        def _(quarter):
-            left = terms[pl.ds(pl.multiple_of(quarter * 2 * rows_total, 2 * rows_total), 2 * rows_total), :]
+                lanes = pl.ds(pl.multiple_of((half * (chan_count // 2) + couple) * LANES, LANES), LANES)
+                for polar, value in enumerate(polars):
+                    turned = pltpu.roll(value, 64, 1) * turn_sign
+                    terms[polar * rows_total : (polar + 1) * rows_total, lanes] = value.astype(jnp.bfloat16)
+                    terms[(2 + polar) * rows_total : (3 + polar) * rows_total, lanes] = turned.astype(jnp.bfloat16)
+
+        for part in range(2):
             out = lax.dot_general(
-                left, terms[:rows_total, :], (((1,), (1,)), ((), ())), preferred_element_type=jnp.float32
-            ).astype(jnp.bfloat16)
-            for which in range(2):
-                rows = out[which * rows_total : (which + 1) * rows_total]
-                b_src[own, :, 2 * quarter + which] = rows.reshape(stn_count, stations, rows_total)
-            for which in range(2):
+                terms[part * 2 * rows_total : (part + 1) * 2 * rows_total, :], terms[: 2 * rows_total, :],
+                (((1,), (1,)), ((), ())), preferred_element_type=jnp.float32,
+            )
+            xx, xy = out[:rows_total, :rows_total], out[:rows_total, rows_total:]
+            yx, yy = out[rows_total:, :rows_total], out[rows_total:, rows_total:]
+            stokes = [
+                (part, xx + yy), (2 + part, xx - yy), (4 + part, xy + yx),
+                (7, yx - xy) if part == 0 else (6, xy - yx),
+            ]
+            for index, value in stokes:
+                b_src[own, :, index] = value.astype(jnp.bfloat16).reshape(stn_count, stations, rows_total)
+            for index, _ in stokes:
                 for target in targets:
                     pltpu.make_async_remote_copy(
-                        src_ref=b_src.at[own, target, 2 * quarter + which],
-                        dst_ref=out_ref.at[stn * per_device + own, 2 * quarter + which],
+                        src_ref=b_src.at[own, target, index],
+                        dst_ref=out_ref.at[stn * per_device + own, index],
                         send_sem=b_send, recv_sem=b_recv, device_id=(target, chan), device_id_type=MESH,
                     ).start()
 
@@ -331,7 +350,7 @@
             vmem((2 * count * stations, LANES), jnp.float32),
             vmem((per_device, count, 2 * stations, LANES), jnp.bfloat16),
             vmem((per_device, count, 2 * stations, LANES), jnp.bfloat16),
-            vmem((8 * total, 2 * chan_count * LANES), jnp.bfloat16),
+            vmem((4 * total, chan_count * LANES), jnp.bfloat16),
             vmem((per_device, stn_count, 8, stations, total), jnp.bfloat16),
             vmem(((TAPS - 1) * feeds, width), jnp.bfloat16),
             vmem(((TAPS - 1) * feeds, width), jnp.bfloat16),

time: 114 us -> 114 us (level)
  no operation moved by 1% of the time
where the time goes in v4:
time: 114 us; the launch traced here: 113 us
  Pallas kernels  113 us (99%)
    pallas_call x1, Pallas kernels, on_device(): pl.pallas_call(kernel, out_shape=vmem(out_dims, jnp.bfloat16), in_specs=[...  110 us
    pallas_call x1, Pallas kernels, on_device(): pl.pallas_call(functools.partial(widen, 1.0 / (steps * chan_count)), out_...  3.46 us

profile of v4, /device:TPU:1, one launch (start us, length us, event | category | flops | bytes accessed | tf_op | source)
XLA Modules:
  0.0 113.4 jit_solution(5955249365786420961)
XLA Ops:
  0.0 110.0 %correlate.1.narrow = bf16[64,8,16,256]{3,2,1,0:T(8,128)(2,1)S(1)} custom-call(bf16[32,64,1024]{2,1,0:T(8,128)(2,1)} %bitcast.1, f32[4,512]{1,0:T(4,128)} %taps_ref.1, s32[16]{0:T(128)} %flags_ref.1, bf16[512,1024]{1,0:T(8,128)(2,1)} %constant.2.clone.table_hbm), custom_call_target="tpu_custom_call" | custom-call | tf_op jit(solution)/shard_map/correlate/pallas_call | solution.py:335
  110.0 3.5 %widen.1 = f32[64,8,16,256]{3,2,1,0:T(8,128)} custom-call(bf16[64,8,16,256]{3,2,1,0:T(8,128)(2,1)S(1)} %correlate.1.narrow), custom_call_target="tpu_custom_call" | custom-call | tf_op jit(solution)/shard_map/widen/pallas_call | solution.py:371

commit v5 on v4

--- a/solution.py
+++ b/solution.py
@@ -29,8 +29,8 @@
 
 
 def kernel(
-    volt_hbm, taps_ref, flags_ref, table_hbm, out_ref,
-    volt, table, raw, mixed, planes, a_src, a_dst, terms, b_src, halo_src, halo_dst,
+    volt_hbm, taps_hbm, flags_hbm, table_hbm, out_ref,
+    taps_ref, flags_ref, volt, table, raw, mixed_even, mixed_odd, planes, a_src, a_dst, terms, b_src, halo_src, halo_dst,
     load_sem, halo_send, halo_recv, a_send, a_recv, b_send, b_recv, own_sem,
 ):
     stn_count, chan_count = lax.axis_size("stn"), lax.axis_size("chan")
@@ -41,7 +41,7 @@
     stations = feeds // 2
     pitch = steps + 8
     per_device = CHANNELS // count
-    parts = load_sem.shape[0] - 1
+    parts = load_sem.shape[0] - 3
     share = feeds // parts
 
     def owner(index):
@@ -73,6 +73,12 @@
         span = pl.ds(part * share, share)
         loads.append(pltpu.make_async_copy(volt_hbm.at[span], volt.at[span], load_sem.at[part]))
         loads[-1].start()
+    small_copies = [
+        pltpu.make_async_copy(taps_hbm, taps_ref, load_sem.at[parts + 1]),
+        pltpu.make_async_copy(flags_hbm, flags_ref, load_sem.at[parts + 2]),
+    ]
+    for copy in small_copies:
+        copy.start()
     table_copy.start()
 
     barrier = pltpu.get_barrier_semaphore()
@@ -82,25 +88,32 @@
 
     each_partner(greet)
 
-    for part in range(parts):
-        loads[part].wait()
-
-        @pl.loop(part * share, (part + 1) * share)
-        def _(feed):
-            flag = flags_ref[feed // 2].astype(jnp.float32)
-            for tile in range(8):
-                block = volt[feed, :, tile * LANES : (tile + 1) * LANES].astype(jnp.float32) * flag
-                raw[tile, pl.ds(pl.multiple_of(feed * pitch + 8, 8), steps), :] = block
+    for copy in loads + small_copies:
+        copy.wait()
+
+    def widened(feed, start, rows):
+        flag = flags_ref[feed // 2].astype(jnp.float32)
+        for tile in range(8):
+            block = volt[feed, start : start + rows, tile * LANES : (tile + 1) * LANES].astype(jnp.float32)
+            raw[tile, pl.ds(pl.multiple_of(feed * pitch + 8 + start, 8), rows), :] = block * flag
+
+    @pl.loop(0, feeds)
+    def _(feed):
+        widened(feed, steps - 16, 16)
 
     for tile in range(8):
         for back in range(TAPS - 1):
             rows = raw[tile, pl.ds(8 + steps - (TAPS - 1) + back, feeds, stride=pitch), :]
             halo_src[pl.ds(back * feeds, feeds), pl.ds(tile * LANES, LANES)] = rows.astype(jnp.bfloat16)
 
-    def filtered(half, both):
+    mixed_of = (mixed_even, mixed_odd)
+
+    def filtered(half, both, odd):
         first = 4 - 4 * half
         for feed_of in range(4):
             feed = 4 * both + feed_of
+            if half == 0:
+                widened(feed, 0, steps - 16)
             for tile in range(8):
                 weights = [
                     taps_ref[pl.ds(tap, 1), pl.ds((tile % 4) * LANES, LANES)] for tap in range(TAPS)
@@ -116,20 +129,20 @@
                         total = total + weights[tap] * rows[index + tap]
                     sums.append(total)
                 block = jnp.concatenate(sums, axis=0).astype(jnp.bfloat16)
-                base = both * 2 * LANES + feed_of // 2 * LANES + feed_of % 2 * 32
-                mixed[
+                base = both // 2 * 2 * LANES + feed_of // 2 * LANES + feed_of % 2 * 32
+                mixed_of[odd][
                     half, pl.ds(pl.multiple_of(base, 32), 32), tile * LANES : (tile + 1) * LANES
                 ] = block
                 other = (tile + 4) % 8
                 turned = block if tile >= 4 else -block
-                mixed[
+                mixed_of[odd][
                     half, pl.ds(pl.multiple_of(base + 64, 32), 32), other * LANES : (other + 1) * LANES
                 ] = turned
 
     depth = 2 * stations
 
-    def transformed(half, pair, both):
-        rows = mixed[half, pl.ds(pl.multiple_of(both * 256, 256), 256), :]
+    def transformed(half, pair, both, odd):
+        rows = mixed_of[odd][half, pl.ds(pl.multiple_of(both // 2 * 256, 256), 256), :]
         out = lax.dot_general(
             table[pair * 2 * count : (pair + 1) * 2 * count, :], rows,
             (((1,), (1,)), ((), ())), preferred_element_type=jnp.float32,
@@ -148,20 +161,24 @@
 
     def first_spectra(half):
         last = stations // 2 - 1
-        filtered(half, 0)
-
-        @pl.loop(0, last)
-        def _(both):
-            transformed(half, 0, both)
-            filtered(half, both + 1)
-
-        transformed(half, 0, last)
+        filtered(half, 0, 0)
+
+        @pl.loop(0, last // 2)
+        def _(step):
+            for odd in range(2):
+                transformed(half, 0, 2 * step + odd, odd)
+                filtered(half, 2 * step + odd + 1, 1 - odd)
+
+        transformed(half, 0, last - 1, 0)
+        filtered(half, last, 1)
+        transformed(half, 0, last, 1)
         packed(half, 0)
 
     def second_spectra(half):
-        @pl.loop(0, stations // 2)
-        def _(both):
-            transformed(half, 1, both)
+        @pl.loop(0, stations // 4)
+        def _(step):
+            for odd in range(2):
+                transformed(half, 1, 2 * step + odd, odd)
 
         packed(half, 1)
 
@@ -337,16 +354,19 @@
         out_shape=vmem(out_dims, jnp.bfloat16),
         in_specs=[
             pl.BlockSpec(memory_space=pltpu.HBM),
-            pl.BlockSpec(memory_space=vmem),
-            pl.BlockSpec(memory_space=pltpu.SMEM),
+            pl.BlockSpec(memory_space=pltpu.HBM),
+            pl.BlockSpec(memory_space=pltpu.HBM),
             pl.BlockSpec(memory_space=pltpu.HBM),
         ],
         out_specs=pl.BlockSpec(memory_space=vmem),
         scratch_shapes=[
+            vmem(taps.shape, jnp.float32),
+            pltpu.SMEM(flags.shape, jnp.int32),
             vmem((feeds, steps, width), jnp.bfloat16),
             vmem((CHANNELS, width), jnp.bfloat16),
             vmem((8, feeds * (steps + 8), LANES), jnp.float32),
-            vmem((2, stations * LANES, width), jnp.bfloat16),
+            vmem((2, stations // 2 * LANES, width), jnp.bfloat16),
+            vmem((2, stations // 2 * LANES, width), jnp.bfloat16),
             vmem((2 * count * stations, LANES), jnp.float32),
             vmem((per_device, count, 2 * stations, LANES), jnp.bfloat16),
             vmem((per_device, count, 2 * stations, LANES), jnp.bfloat16),
@@ -354,7 +374,7 @@
             vmem((per_device, stn_count, 8, stations, total), jnp.bfloat16),
             vmem(((TAPS - 1) * feeds, width), jnp.bfloat16),
             vmem(((TAPS - 1) * feeds, width), jnp.bfloat16),
-            pltpu.SemaphoreType.DMA((5,)),
+            pltpu.SemaphoreType.DMA((7,)),
             pltpu.SemaphoreType.DMA((TAPS - 1,)),
             pltpu.SemaphoreType.DMA((TAPS - 1,)),
             pltpu.SemaphoreType.DMA((per_device,)),

time: 114 us -> 113 us (level)
  no operation moved by 1% of the time
where the time goes in v5:
time: 113 us
  Pallas kernels  112 us (99%)
    pallas_call x1, Pallas kernels, on_device(): pl.pallas_call(kernel, out_shape=vmem(out_dims, jnp.bfloat16), in_specs=[...  109 us
    pallas_call x1, Pallas kernels, on_device(): pl.pallas_call(functools.partial(widen, 1.0 / (steps * chan_count)), out_...  3.46 us

profile of v5, /device:TPU:1, one launch (start us, length us, event | category | flops | bytes accessed | tf_op | source)
XLA Modules:
  0.0 112.6 jit_solution(4794041102516245536)
XLA Ops:
  0.0 109.0 %correlate.1.narrow = bf16[64,8,16,256]{3,2,1,0:T(8,128)(2,1)S(1)} custom-call(bf16[32,64,1024]{2,1,0:T(8,128)(2,1)} %bitcast.1, f32[4,512]{1,0:T(4,128)} %taps_hbm.1, s32[16]{0:T(128)} %flags_hbm.1, bf16[512,1024]{1,0:T(8,128)(2,1)} %constant.2.clone.table_hbm), custom_call_target="tpu_custom_call" | custom-call | tf_op jit(solution)/shard_map/correlate/pallas_call | solution.py:352
  109.0 3.5 %widen.1 = f32[64,8,16,256]{3,2,1,0:T(8,128)} custom-call(bf16[64,8,16,256]{3,2,1,0:T(8,128)(2,1)S(1)} %correlate.1.narrow), custom_call_target="tpu_custom_call" | custom-call | tf_op jit(solution)/shard_map/widen/pallas_call | solution.py:391

commit v6 on v5

--- a/solution.py
+++ b/solution.py
@@ -150,14 +150,9 @@
         planes[pl.ds(2 * both, 2 * count, stride=stations), :] = out[:, :LANES]
         planes[pl.ds(2 * both + 1, 2 * count, stride=stations), :] = out[:, LANES:]
 
-    def packed(half, pair):
-        group = 16
-        slot = 2 * pair + half
-
-        @pl.loop(0, count // group)
-        def _(block):
-            rows = planes[pl.ds(pl.multiple_of(block * (group * depth), group * depth), group * depth), :]
-            a_src[slot, pl.ds(block * group, group)] = rows.astype(jnp.bfloat16).reshape(group, depth, LANES)
+    def packed(index):
+        rows = planes[pl.ds(pl.multiple_of(index * depth, depth), depth), :]
+        return rows.astype(jnp.bfloat16)
 
     def first_spectra(half):
         last = stations // 2 - 1
@@ -172,7 +167,6 @@
         transformed(half, 0, last - 1, 0)
         filtered(half, last, 1)
         transformed(half, 0, last, 1)
-        packed(half, 0)
 
     def second_spectra(half):
         @pl.loop(0, stations // 4)
@@ -180,28 +174,27 @@
             for odd in range(2):
                 transformed(half, 1, 2 * step + odd, odd)
 
-        packed(half, 1)
-
     def send_spectra(half, pair):
         slot = 2 * pair + half
 
         @each_partner
         def _(index):
+            a_src[slot, index] = packed(index)
             pltpu.make_async_remote_copy(
                 src_ref=a_src.at[slot, index], dst_ref=a_dst.at[slot, me],
                 send_sem=a_send.at[slot], recv_sem=a_recv.at[slot],
                 device_id=owner(index), device_id_type=MESH,
             ).start()
 
-        a_dst[slot, me] = a_src[slot, me]
-
-    def await_spectra(half, pair):
+        a_dst[slot, me] = packed(me)
+
+    def all_spectra(half, pair):
         slot = 2 * pair + half
         ref = a_dst.at[slot, pl.ds(0, count - 1)]
-        pltpu.make_async_remote_copy(
+        return pltpu.make_async_remote_copy(
             src_ref=ref, dst_ref=ref, send_sem=a_send.at[slot], recv_sem=a_recv.at[slot],
             device_id=owner(me), device_id_type=MESH,
-        ).wait()
+        )
 
     pl.semaphore_wait(barrier, count - 1)
 
@@ -221,9 +214,6 @@
     table_copy.wait()
     first_spectra(0)
     send_spectra(0, 0)
-
-    for copy in halo:
-        pl.when(has_next)(copy.wait_send)
 
     @pl.when(has_last)
     def _():
@@ -306,8 +296,8 @@
     own_copies = []
     for own in range(per_device):
         if own % 2 == 0:
-            await_spectra(0, own // 2)
-            await_spectra(1, own // 2)
+            all_spectra(0, own // 2).wait_recv()
+            all_spectra(1, own // 2).wait_recv()
         correlated(own)
 
         own_copies.append(
@@ -315,6 +305,11 @@
         )
         own_copies[-1].start()
 
+    for copy in halo:
+        pl.when(has_next)(copy.wait_send)
+    for pair in range(per_device // 2):
+        for half in range(2):
+            all_spectra(half, pair).wait_send()
     for copy in own_copies:
         copy.wait()
     ref = out_ref.at[pl.ds(0, (stn_count - 1) * per_device)]

time: 113 us -> 113 us (level)
  no operation moved by 1% of the time
where the time goes in v6:
time: 113 us
  Pallas kernels  112 us (99%)
    pallas_call x1, Pallas kernels, on_device(): pl.pallas_call(kernel, out_shape=vmem(out_dims, jnp.bfloat16), in_specs=[...  109 us
    pallas_call x1, Pallas kernels, on_device(): pl.pallas_call(functools.partial(widen, 1.0 / (steps * chan_count)), out_...  3.46 us

profile of v6, /device:TPU:1, one launch (start us, length us, event | category | flops | bytes accessed | tf_op | source)
XLA Modules:
  0.0 112.5 jit_solution(18302037892215031606)
XLA Ops:
  0.0 108.9 %correlate.1.narrow = bf16[64,8,16,256]{3,2,1,0:T(8,128)(2,1)S(1)} custom-call(bf16[32,64,1024]{2,1,0:T(8,128)(2,1)} %bitcast.1, f32[4,512]{1,0:T(4,128)} %taps_hbm.1, s32[16]{0:T(128)} %flags_hbm.1, bf16[512,1024]{1,0:T(8,128)(2,1)} %constant.2.clone.table_hbm), custom_call_target="tpu_custom_call" | custom-call | tf_op jit(solution)/shard_map/correlate/pallas_call | solution.py:347
  108.9 3.5 %widen.1 = f32[64,8,16,256]{3,2,1,0:T(8,128)} custom-call(bf16[64,8,16,256]{3,2,1,0:T(8,128)(2,1)S(1)} %correlate.1.narrow), custom_call_target="tpu_custom_call" | custom-call | tf_op jit(solution)/shard_map/widen/pallas_call | solution.py:386

commit v7 on v6

--- a/solution.py
+++ b/solution.py
@@ -154,16 +154,37 @@
         rows = planes[pl.ds(pl.multiple_of(index * depth, depth), depth), :]
         return rows.astype(jnp.bfloat16)
 
+    halo = []
+    has_next, has_last = chan < chan_count - 1, chan > 0
+
+    def open_links():
+        pl.semaphore_wait(barrier, count - 1)
+
+        for back in range(TAPS - 1):
+            span = pl.ds(back * feeds, feeds)
+            halo.append(
+                pltpu.make_async_remote_copy(
+                    src_ref=halo_src.at[span], dst_ref=halo_dst.at[span],
+                    send_sem=halo_send.at[back], recv_sem=halo_recv.at[back],
+                    device_id=(stn, (chan + 1) % chan_count), device_id_type=MESH,
+                )
+            )
+            pl.when(has_next)(halo[-1].start)
+
     def first_spectra(half):
         last = stations // 2 - 1
         filtered(half, 0, 0)
 
-        @pl.loop(0, last // 2)
-        def _(step):
+        def advance(step):
             for odd in range(2):
                 transformed(half, 0, 2 * step + odd, odd)
                 filtered(half, 2 * step + odd + 1, 1 - odd)
 
+        ahead = 1 if half == 0 else 0
+        pl.loop(0, ahead)(advance)
+        if half == 0:
+            open_links()
+        pl.loop(ahead, last // 2)(advance)
         transformed(half, 0, last - 1, 0)
         filtered(half, last, 1)
         transformed(half, 0, last, 1)
@@ -195,21 +216,6 @@
             src_ref=ref, dst_ref=ref, send_sem=a_send.at[slot], recv_sem=a_recv.at[slot],
             device_id=owner(me), device_id_type=MESH,
         )
-
-    pl.semaphore_wait(barrier, count - 1)
-
-    has_next, has_last = chan < chan_count - 1, chan > 0
-    halo = []
-    for back in range(TAPS - 1):
-        span = pl.ds(back * feeds, feeds)
-        halo.append(
-            pltpu.make_async_remote_copy(
-                src_ref=halo_src.at[span], dst_ref=halo_dst.at[span],
-                send_sem=halo_send.at[back], recv_sem=halo_recv.at[back],
-                device_id=(stn, (chan + 1) % chan_count), device_id_type=MESH,
-            )
-        )
-        pl.when(has_next)(halo[-1].start)
 
     table_copy.wait()
     first_spectra(0)

time: 113 us -> 115 us (1.018)
  Pallas kernels: 112 us -> 115 us
    pallas_call x1, Pallas kernels: 109 us -> 111 us  [on_device(): pl.pallas_call(kernel, out_shape=vmem(out_dims, jnp.bfloat16), in_specs=[...]
where the time goes in v7:
time: 115 us
  Pallas kernels  115 us (100%)
    pallas_call x1, Pallas kernels, on_device(): pl.pallas_call(kernel, out_shape=vmem(out_dims, jnp.bfloat16), in_specs=[...  111 us
    pallas_call x1, Pallas kernels, on_device(): pl.pallas_call(functools.partial(widen, 1.0 / (steps * chan_count)), out_...  3.46 us

profile of v7, /device:TPU:1, one launch (start us, length us, event | category | flops | bytes accessed | tf_op | source)
XLA Modules:
  0.0 115.1 jit_solution(16608532632960635146)
XLA Ops:
  0.0 111.5 %correlate.1.narrow = bf16[64,8,16,256]{3,2,1,0:T(8,128)(2,1)S(1)} custom-call(bf16[32,64,1024]{2,1,0:T(8,128)(2,1)} %bitcast.1, f32[4,512]{1,0:T(4,128)} %taps_hbm.1, s32[16]{0:T(128)} %flags_hbm.1, bf16[512,1024]{1,0:T(8,128)(2,1)} %constant.2.clone.table_hbm), custom_call_target="tpu_custom_call" | custom-call | tf_op jit(solution)/shard_map/correlate/pallas_call | solution.py:353
  111.5 3.5 %widen.1 = f32[64,8,16,256]{3,2,1,0:T(8,128)} custom-call(bf16[64,8,16,256]{3,2,1,0:T(8,128)(2,1)S(1)} %correlate.1.narrow), custom_call_target="tpu_custom_call" | custom-call | tf_op jit(solution)/shard_map/widen/pallas_call | solution.py:392
